TPU v7x, 32 devices: a whole 2x2x4 slice. The times are simulated.
32 devices in a mesh: row: 4 (over z), col: 8 (over y, x, core).
Axes of the slice: x: 2, y: 2, z: 4, core: 2. Of those that a mesh axis runs over, the one named last changes fastest.
Arguments:
- star_pos: float32 [128, 3, 128], P(('row', 'col')), may hold values from -5 to 5
- star_vel: float32 [128, 3, 128], P(('row', 'col')), may hold values from -5 to 5
- star_acc: float32 [128, 3, 128], P(('row', 'col')), may hold values from -5 to 5
- star_jerk: float32 [128, 3, 128], P(('row', 'col')), may hold values from -5 to 5
- star_mass: float32 [128, 128], P(('row', 'col')), may hold values from 0.00012207031 to 0.0009765625
- active_index: int32 [32, 128], P(('row', 'col')), may hold values from 0 to 511, as said below
- send_block: int32 [32, 32, 4], P(('row', 'col')), may hold values from -1 to 3, as said below
- send_leaf: int32 [32, 32, 4], P(('row', 'col')), may hold values from -1 to 127
- galaxy_pos: float32 [4096, 3, 128], P(('row', 'col')), may hold values from -5 to 5
- galaxy_mass: float32 [4096, 128], P(('row', 'col')), may hold values from 0.0001 to 0.001
Outputs:
- star_pos_new: float32 [128, 3, 128], P(('row', 'col'))
- star_vel_new: float32 [128, 3, 128], P(('row', 'col'))
- galaxy_accel: float32 [4096, 3, 128], P(('row', 'col'))
Inputs may be any that keep to these rules, and one draw needn't show every extreme that they name: `active_index`: the entries of one device's row are distinct. `send_block`: an entry is -1 exactly where the same entry of send_leaf is -1. Every device fills all 4 slots to itself, and one device receives 4 filled slots from every device.
All inputs are finite; a program needn't handle non-finite values.
Results may differ from a plain program's by a relative error of at most 0.0003.
Values sent between devices are 32-bit elements; how exact they have to be, the bound alone decides.
A program may use at most 64 MiB of HBM per device.

v0:
```python
import math

import jax
import jax.numpy as jnp
from jax import lax
from jax.sharding import PartitionSpec as P

STAR_DEV = 512
BLOCK = 128


step_length = 1.0
soft_star = 0.01
soft_galaxy = 0.04


def pair_block(apos, avel, rpos, rvel, rmass):
    delta = rpos[:, None, :] - apos[:, :, None]
    dvel = rvel[:, None, :] - avel[:, :, None]
    radius = jnp.sum(delta * delta, 0) + soft_star
    inverse = lax.rsqrt(radius)
    weight = rmass[None, :] * inverse * inverse * inverse
    along = jnp.sum(delta * dvel, 0) * inverse * inverse
    accel = jnp.sum(delta * weight[None], -1)
    jerks = jnp.sum((dvel - 3.0 * along[None] * delta) * weight[None], -1)
    return (accel, jerks)


def pair_terms(piece, rpos, rvel, rmass):
    count = piece.shape[1]
    size = math.gcd(count, 512)
    grouped = piece.reshape(6, count // size, size).transpose(1, 0, 2)

    def pair_one(item):
        accel, jerks = pair_block(item[:3], item[3:], rpos, rvel, rmass)
        return jnp.concatenate([accel, jerks], 0)

    result = lax.map(pair_one, grouped)
    return result.transpose(1, 0, 2).reshape(6, count)


def entry_terms(stars4, leaves4):
    count = stars4.shape[0]
    group = math.gcd(count, 16)

    def entry_one(item):
        spos = item[0][:, :3]
        smass = item[0][:, 3]
        gpos = item[1][:, :3]
        gmass = item[1][:, 3]
        delta = gpos[:, :, None, :] - spos[:, :, :, None]
        radius = jnp.sum(delta * delta, 1) + soft_galaxy
        inverse = lax.rsqrt(radius)
        cube = inverse * inverse * inverse
        kick = jnp.sum(delta * (gmass[:, None, :] * cube)[:, None], -1)
        pull = -jnp.sum(delta * (smass[:, :, None] * cube)[:, None], 2)
        return (pull, kick)

    shaped = (
        stars4.reshape((count // group, group) + stars4.shape[1:]),
        leaves4.reshape((count // group, group) + leaves4.shape[1:]),
    )
    pull, kick = lax.map(entry_one, shaped)
    return (pull.reshape((count,) + pull.shape[2:]), kick.reshape((count,) + kick.shape[2:]))


def flatten(blocks):
    return blocks.transpose(1, 0, 2).reshape(3, -1)


def local(
    star_pos,
    star_vel,
    star_acc,
    star_jerk,
    star_mass,
    active_index,
    send_block,
    send_leaf,
    galaxy_pos,
    galaxy_mass,
):
    nblock = star_pos.shape[0]
    width = star_pos.shape[2]
    half = 0.5 * step_length**2
    sixth = step_length**3 / 6.0
    pred_pos = star_pos + step_length * star_vel + half * star_acc + sixth * star_jerk
    pred_vel = star_vel + step_length * star_acc + half * star_jerk
    pos_flat = flatten(pred_pos)
    vel_flat = flatten(pred_vel)
    mass_flat = star_mass.reshape(-1)
    chosen = active_index[0]
    active = jnp.concatenate([pos_flat[:, chosen], vel_flat[:, chosen]], 0)
    res_pos, res_vel, res_mass = (
        lax.all_gather(pos_flat, "row", axis=1, tiled=True),
        lax.all_gather(vel_flat, "row", axis=1, tiled=True),
        lax.all_gather(mass_flat, "row", axis=0, tiled=True),
    )
    terms = pair_terms(
        lax.all_gather(active, "col", axis=1, tiled=True), res_pos, res_vel, res_mass
    )
    forces = lax.psum_scatter(terms, "col", scatter_dimension=1, tiled=True)
    acc_new = forces[:3]
    jerk_new = forces[3:]
    start_acc = flatten(star_acc)[:, chosen]
    start_jerk = flatten(star_jerk)[:, chosen]
    start_pos = flatten(star_pos)[:, chosen]
    start_vel = flatten(star_vel)[:, chosen]
    vel_one = (
        start_vel
        + (start_acc + acc_new) * (0.5 * step_length)
        + (start_jerk - jerk_new) * (step_length**2 / 12.0)
    )
    pos_one = (
        start_pos
        + (start_vel + vel_one) * (0.5 * step_length)
        + (start_acc - acc_new) * (step_length**2 / 12.0)
    )
    pos_new = pos_flat.at[:, chosen].set(pos_one).reshape(3, nblock, width).transpose(1, 0, 2)
    vel_mid = vel_flat.at[:, chosen].set(vel_one).reshape(3, nblock, width).transpose(1, 0, 2)
    table = send_block[0]
    targets = table.shape[0]
    slots = table.shape[1]
    entries = targets * slots
    pick = (
        (table[:, :, None] == jnp.arange(nblock, dtype=jnp.int32))
        .astype(jnp.float32)
        .reshape(entries, nblock)
    )
    packed = jnp.concatenate([pos_new, star_mass[:, None, :]], 1).reshape(nblock, -1)
    outgoing = jnp.dot(
        pick, packed, precision=lax.Precision.HIGHEST, preferred_element_type=jnp.float32
    )
    outgoing = outgoing.reshape(targets, slots, 4, width)
    rows = lax.axis_size("row")
    cols = lax.axis_size("col")
    arrived, arrived_leaf = (
        lax.all_to_all(outgoing, ("row", "col"), split_axis=0, concat_axis=0, tiled=True),
        lax.all_to_all(send_leaf[0], ("row", "col"), split_axis=0, concat_axis=0, tiled=True),
    )
    leaves = galaxy_pos.shape[0]
    depth = galaxy_pos.shape[2]
    grab = (arrived_leaf.reshape(entries)[:, None] == jnp.arange(leaves, dtype=jnp.int32)).astype(
        jnp.float32
    )
    packed_gal = jnp.concatenate([galaxy_pos, galaxy_mass[:, None, :]], 1).reshape(leaves, -1)
    local_leaves = jnp.dot(
        grab, packed_gal, precision=lax.Precision.HIGHEST, preferred_element_type=jnp.float32
    )
    pull, kick = entry_terms(
        arrived.reshape(entries, 4, width), local_leaves.reshape(entries, 4, depth)
    )
    pull_total = lax.dot_general(
        grab,
        pull.reshape(entries, -1),
        (((0,), (0,)), ((), ())),
        precision=lax.Precision.HIGHEST,
        preferred_element_type=jnp.float32,
    )
    galaxy_accel = pull_total.reshape(leaves, 3, depth) * (STAR_DEV * rows * cols / BLOCK)
    returned = lax.all_to_all(
        kick.reshape(targets, slots, 3, width),
        ("row", "col"),
        split_axis=0,
        concat_axis=0,
        tiled=True,
    )
    kick_blocks = lax.dot_general(
        pick,
        returned.reshape(entries, -1),
        (((0,), (0,)), ((), ())),
        precision=lax.Precision.HIGHEST,
        preferred_element_type=jnp.float32,
    )
    star_vel_new = vel_mid + step_length * kick_blocks.reshape(nblock, 3, width)
    return (pos_new, star_vel_new, galaxy_accel)


def solution(mesh):
    return jax.shard_map(
        local,
        mesh=mesh,
        in_specs=(
            P(("row", "col"), None, None),
            P(("row", "col"), None, None),
            P(("row", "col"), None, None),
            P(("row", "col"), None, None),
            P(("row", "col"), None),
            P(("row", "col"), None),
            P(("row", "col"), None, None),
            P(("row", "col"), None, None),
            P(("row", "col"), None, None),
            P(("row", "col"), None),
        ),
        out_specs=(
            P(("row", "col"), None, None),
            P(("row", "col"), None, None),
            P(("row", "col"), None, None),
        ),
        check_vma=False,
    )
```

profile of v0, /device:TPU:1, one launch (start us, length us, event | category | flops | bytes accessed | tf_op | source)
XLA Modules:
  0.0 195.0 jit_solution(615105160131119341)
XLA Ops:
  7.2 0.7 fusion.39
  7.9 0.7 add_bitcast_fusion
  8.8 21.0 %all_gather.12 = f32[3,2048]{0,1:T(8,128)S(1)} all-gather(f32[3,512]{0,1:T(8,128)S(1)} %bitcast.185), channel_id=1, replica_groups=mesh['row'=4,'col'=8] {'row'}, dimensions={1}, use_global_device_ids=true | all-gather | bytes 30720 | tf_op jit(solution)/shard_map/all_gather | solution.py:95
  30.6 0.6 gather_fusion.4
  31.2 19.4 %all_gather.15 = f32[3,2048]{0,1:T(8,128)S(1)} all-gather(f32[3,512]{0,1:T(8,128)S(1)} %bitcast.182), channel_id=1, replica_groups=mesh['row'=4,'col'=8] {'row'}, dimensions={1}, use_global_device_ids=true | all-gather | bytes 30720 | tf_op jit(solution)/shard_map/all_gather | solution.py:96
  50.8 14.5 %all_gather.13 = f32[6,1024]{1,0:T(8,128)S(1)} all-gather(f32[6,128]{1,0:T(8,128)S(1)} %pad_maximum_fusion), channel_id=1, replica_groups=mesh['row'=4,'col'=8] {'col'}, dimensions={1}, use_global_device_ids=true | all-gather | bytes 27648 | tf_op jit(solution)/shard_map/all_gather | solution.py:100
  66.0 9.3 %all-gather = f32[4,1,512]{2,1,0:T(1,128)S(1)} all-gather(f32[1,1,512]{2,1,0:T(1,128)S(1)} %bitcast.214), channel_id=1, replica_groups=mesh['row'=4,'col'=8] {'row'}, dimensions={0}, use_global_device_ids=true | all-gather | bytes 10240 | tf_op jit(solution)/shard_map/all_gather | solution.py:97
  75.3 19.9 %while.22 = (s32[]{:T(128)}, f32[2,6,512]{2,1,0:T(8,128)S(1)}, f32[3,2048]{1,0:T(4,128)S(1)}, f32[2,6,512]{2,1,0:T(8,128)S(1)}, f32[2048]{0:T(1024)S(1)}, /*inde...) while((s32[]{:T(128)}, f32[2,6,512]{2,1,0:T(8,128)S(1)}, f32[3,2048]{1,0:T(4,128)S(1)}, ...), condition=%wide.region_5.6_spmd, body=%wide.region_0.5_spmd.sunk | while | flops 49283072 | bytes 33755252 | solution.py:38
  75.4 3.6 %fusion.52 = (f32[512,2048]{1,0:T(8,128)S(1)}, f32[512,2048]{1,0:T(8,128)S(1)}) fusion(f32[3,512]{1,0:T(4,128)S(1)} %get-tuple-element.260, f32[3,2048]{1,0:T(4,128)S(1)} %get-tuple-element.299, f32[3,512]{1,0:T(4,128)S(1)} %get-tuple-element.261, f32[3,2048]{1,0:T(4,128)S(1)} %get-tuple-element.302), kind=kLoop, calls=%fused_computation.15.clone.1 | loop fusion | flops 16777216 | bytes 8450048 | tf_op jit(solution)/shard_map/while/body/eval_jaxpr/reduce_sum | solution.py:20
  79.0 1.9 fusion.53
  81.0 4.3 %fusion.54 = (f32[3,512]{1,0:T(4,128)S(1)}, f32[3,512]{1,0:T(4,128)S(1)}) fusion(f32[512,2048]{1,0:T(8,128)S(1)} %get-tuple-element.264, f32[3,512]{1,0:T(4,128)S(1)} %get-tuple-element.260, f32[3,2048]{1,0:T(4,128)S(1)} %get-tuple-element.299, f32[512,2048]{1,0:T(8,128)S(1)} %get-tuple-element.265, f32[3,512]{1,0:T(4,128)S(1)} %get-tuple-element.261, ...), kind=kLoop, calls=%fused_computation.16.clone.1 | loop fusion | flops 25162752 | bytes 8462336 | tf_op jit(solution)/shard_map/while/body/eval_jaxpr/reduce_sum | solution.py:24
  85.3 3.6 %fusion.52 = (f32[512,2048]{1,0:T(8,128)S(1)}, f32[512,2048]{1,0:T(8,128)S(1)}) fusion(f32[3,512]{1,0:T(4,128)S(1)} %get-tuple-element.260, f32[3,2048]{1,0:T(4,128)S(1)} %get-tuple-element.299, f32[3,512]{1,0:T(4,128)S(1)} %get-tuple-element.261, f32[3,2048]{1,0:T(4,128)S(1)} %get-tuple-element.302), kind=kLoop, calls=%fused_computation.15.clone.1 | loop fusion | flops 16777216 | bytes 8450048 | tf_op jit(solution)/shard_map/while/body/eval_jaxpr/reduce_sum | solution.py:20
  89.0 1.9 fusion.53
  90.9 4.3 %fusion.54 = (f32[3,512]{1,0:T(4,128)S(1)}, f32[3,512]{1,0:T(4,128)S(1)}) fusion(f32[512,2048]{1,0:T(8,128)S(1)} %get-tuple-element.264, f32[3,512]{1,0:T(4,128)S(1)} %get-tuple-element.260, f32[3,2048]{1,0:T(4,128)S(1)} %get-tuple-element.299, f32[512,2048]{1,0:T(8,128)S(1)} %get-tuple-element.265, f32[3,512]{1,0:T(4,128)S(1)} %get-tuple-element.261, ...), kind=kLoop, calls=%fused_computation.16.clone.1 | loop fusion | flops 25162752 | bytes 8462336 | tf_op jit(solution)/shard_map/while/body/eval_jaxpr/reduce_sum | solution.py:24
  95.9 0.7 copy.177
  96.6 4.9 %all-to-all-start = ((s32[32,1,4]{2,1,0:T(1,128)}), s32[32,1,4]{2,1,0:T(1,128)S(1)}, u32[]{:S(2)}, u32[]{:S(2)}) async-start(s32[32,1,4]{2,1,0:T(1,128)} %copy.177), calls=%async_computation.1 | async-start | bytes 32768 | tf_op jit(solution)/shard_map/all_to_all | solution.py:139
  101.6 0.7 gather_fusion
  104.3 0.6 gather_fusion.5
  105.0 21.6 %reduce-scatter.2.cloned.1.call-done = f32[6,128]{1,0:T(8,128)} async-done(((f32[6,1024]{1,0:T(8,128)}), f32[6,128]{1,0:T(8,128)}) %reduce-scatter.2.cloned.1.call-update) | async-done | bytes 3088 | tf_op jit(solution)/shard_map/reduce_scatter | solution.py:102
  126.6 0.8 fusion.42
  127.5 1.0 scatter_fusion
  128.9 0.9 copy.180
  129.8 5.5 %all-to-all-start.1 = ((f32[32,4,4,128]{3,2,1,0:T(4,128)}), f32[32,4,4,128]{3,2,1,0:T(4,128)S(1)}, u32[]{:S(2)}, u32[]{:S(2)}) async-start(f32[32,4,4,128]{3,2,1,0:T(4,128)} %copy.180), calls=%async_computation.2 | async-start | bytes 524288 | tf_op jit(solution)/shard_map/all_to_all | solution.py:138
  136.1 0.7 reduce.5
  137.2 8.4 %all-to-all-done.1 = f32[32,4,4,128]{3,2,1,0:T(4,128)S(1)} async-done(((f32[32,4,4,128]{3,2,1,0:T(4,128)}), f32[32,4,4,128]{3,2,1,0:T(4,128)S(1)}, u32[]{:S(2)}, u32[]{:S(2)}) %all-to-all-start.1) | async-done | bytes 262176 | tf_op jit(solution)/shard_map/all_to_all | solution.py:138
  145.6 28.7 %while.23 = (s32[]{:T(128)}, f32[8,16,3,128]{3,2,1,0:T(4,128)S(1)}, f32[8,16,3,128]{3,2,1,0:T(4,128)S(1)}, f32[8,16,4,128]{3,1,2,0:T(8,128)S(1)}, f32[8,16,4,128]{3,2,1,0:T(4,128)S(1)}, /*index=5*/s32[]{:T(128)}) while((s32[]{:T(128)}, f32[8,16,3,128]{3,2,1,0:T(4,128)S(1)}, f32[8,16,3,128]{3,2,1,0:T(4,128)S(1)}, ...), condition=%wide.region_13.14_spmd, body=%wide.region_9.13_spmd.sunk | while | flops 7333890 | bytes 7012433 | solution.py:63
  145.7 1.0 fusion.56
  147.1 2.0 %fusion.58 = (f32[16,3,128]{2,1,0:T(4,128)S(1)}, f32[16,3,128]{2,1,0:T(4,128)S(1)}) fusion(f32[16,128,128]{2,1,0:T(8,128)S(1)} %get-tuple-element.273, f32[16,3,128]{2,1,0:T(4,128)S(1)} %copy.208, f32[16,3,128]{2,1,0:T(4,128)S(1)} %copy.209, f32[16,128,128]{2,1,0:T(8,128)S(1)} %get-tuple-element.274), kind=kLoop, calls=%fused_computation.31.clone.1 | loop fusion | flops 3919872 | bytes 2195456 | tf_op jit(solution)/shard_map/while/body/eval_jaxpr/reduce_sum | solution.py:55
  149.2 1.0 fusion.56
  150.7 2.0 %fusion.58 = (f32[16,3,128]{2,1,0:T(4,128)S(1)}, f32[16,3,128]{2,1,0:T(4,128)S(1)}) fusion(f32[16,128,128]{2,1,0:T(8,128)S(1)} %get-tuple-element.273, f32[16,3,128]{2,1,0:T(4,128)S(1)} %copy.208, f32[16,3,128]{2,1,0:T(4,128)S(1)} %copy.209, f32[16,128,128]{2,1,0:T(8,128)S(1)} %get-tuple-element.274), kind=kLoop, calls=%fused_computation.31.clone.1 | loop fusion | flops 3919872 | bytes 2195456 | tf_op jit(solution)/shard_map/while/body/eval_jaxpr/reduce_sum | solution.py:55
  152.8 1.0 fusion.56
  154.3 2.0 %fusion.58 = (f32[16,3,128]{2,1,0:T(4,128)S(1)}, f32[16,3,128]{2,1,0:T(4,128)S(1)}) fusion(f32[16,128,128]{2,1,0:T(8,128)S(1)} %get-tuple-element.273, f32[16,3,128]{2,1,0:T(4,128)S(1)} %copy.208, f32[16,3,128]{2,1,0:T(4,128)S(1)} %copy.209, f32[16,128,128]{2,1,0:T(8,128)S(1)} %get-tuple-element.274), kind=kLoop, calls=%fused_computation.31.clone.1 | loop fusion | flops 3919872 | bytes 2195456 | tf_op jit(solution)/shard_map/while/body/eval_jaxpr/reduce_sum | solution.py:55
  156.4 1.0 fusion.56
  157.9 2.0 %fusion.58 = (f32[16,3,128]{2,1,0:T(4,128)S(1)}, f32[16,3,128]{2,1,0:T(4,128)S(1)}) fusion(f32[16,128,128]{2,1,0:T(8,128)S(1)} %get-tuple-element.273, f32[16,3,128]{2,1,0:T(4,128)S(1)} %copy.208, f32[16,3,128]{2,1,0:T(4,128)S(1)} %copy.209, f32[16,128,128]{2,1,0:T(8,128)S(1)} %get-tuple-element.274), kind=kLoop, calls=%fused_computation.31.clone.1 | loop fusion | flops 3919872 | bytes 2195456 | tf_op jit(solution)/shard_map/while/body/eval_jaxpr/reduce_sum | solution.py:55
  160.0 1.0 fusion.56
  161.5 2.0 %fusion.58 = (f32[16,3,128]{2,1,0:T(4,128)S(1)}, f32[16,3,128]{2,1,0:T(4,128)S(1)}) fusion(f32[16,128,128]{2,1,0:T(8,128)S(1)} %get-tuple-element.273, f32[16,3,128]{2,1,0:T(4,128)S(1)} %copy.208, f32[16,3,128]{2,1,0:T(4,128)S(1)} %copy.209, f32[16,128,128]{2,1,0:T(8,128)S(1)} %get-tuple-element.274), kind=kLoop, calls=%fused_computation.31.clone.1 | loop fusion | flops 3919872 | bytes 2195456 | tf_op jit(solution)/shard_map/while/body/eval_jaxpr/reduce_sum | solution.py:55
  163.6 1.0 fusion.56
  165.1 2.0 %fusion.58 = (f32[16,3,128]{2,1,0:T(4,128)S(1)}, f32[16,3,128]{2,1,0:T(4,128)S(1)}) fusion(f32[16,128,128]{2,1,0:T(8,128)S(1)} %get-tuple-element.273, f32[16,3,128]{2,1,0:T(4,128)S(1)} %copy.208, f32[16,3,128]{2,1,0:T(4,128)S(1)} %copy.209, f32[16,128,128]{2,1,0:T(8,128)S(1)} %get-tuple-element.274), kind=kLoop, calls=%fused_computation.31.clone.1 | loop fusion | flops 3919872 | bytes 2195456 | tf_op jit(solution)/shard_map/while/body/eval_jaxpr/reduce_sum | solution.py:55
  167.2 1.0 fusion.56
  168.7 2.0 %fusion.58 = (f32[16,3,128]{2,1,0:T(4,128)S(1)}, f32[16,3,128]{2,1,0:T(4,128)S(1)}) fusion(f32[16,128,128]{2,1,0:T(8,128)S(1)} %get-tuple-element.273, f32[16,3,128]{2,1,0:T(4,128)S(1)} %copy.208, f32[16,3,128]{2,1,0:T(4,128)S(1)} %copy.209, f32[16,128,128]{2,1,0:T(8,128)S(1)} %get-tuple-element.274), kind=kLoop, calls=%fused_computation.31.clone.1 | loop fusion | flops 3919872 | bytes 2195456 | tf_op jit(solution)/shard_map/while/body/eval_jaxpr/reduce_sum | solution.py:55
  170.8 1.0 fusion.56
  172.3 2.0 %fusion.58 = (f32[16,3,128]{2,1,0:T(4,128)S(1)}, f32[16,3,128]{2,1,0:T(4,128)S(1)}) fusion(f32[16,128,128]{2,1,0:T(8,128)S(1)} %get-tuple-element.273, f32[16,3,128]{2,1,0:T(4,128)S(1)} %copy.208, f32[16,3,128]{2,1,0:T(4,128)S(1)} %copy.209, f32[16,128,128]{2,1,0:T(8,128)S(1)} %get-tuple-element.274), kind=kLoop, calls=%fused_computation.31.clone.1 | loop fusion | flops 3919872 | bytes 2195456 | tf_op jit(solution)/shard_map/while/body/eval_jaxpr/reduce_sum | solution.py:55
  174.3 0.7 copy.184
  175.0 2.8 %all-to-all-start.2 = ((f32[32,4,3,128]{3,1,2,0:T(4,128)}), f32[32,4,3,128]{3,1,2,0:T(4,128)S(1)}, u32[]{:S(2)}, u32[]{:S(2)}) async-start(f32[32,4,3,128]{3,1,2,0:T(4,128)} %copy.184), calls=%async_computation.3 | async-start | bytes 393216 | tf_op jit(solution)/shard_map/all_to_all | solution.py:161
  178.2 1.0 scatter_fusion.1
  179.5 1.0 convolution_multiply_fusion
  180.4 6.7 %all-to-all-done.2 = f32[32,4,3,128]{3,1,2,0:T(4,128)S(1)} async-done(((f32[32,4,3,128]{3,1,2,0:T(4,128)}), f32[32,4,3,128]{3,1,2,0:T(4,128)S(1)}, u32[]{:S(2)}, u32[]{:S(2)}) %all-to-all-start.2) | async-done | bytes 196640 | tf_op jit(solution)/shard_map/all_to_all | solution.py:161
  187.4 0.8 convolution_add_fusion
  (157 shorter events, 11.2 us)
Async XLA Ops:
  7.2 58.8 %copy-start.8 = (f32[4,128]{1,0:T(4,128)S(1)}, f32[4,128]{1,0:T(4,128)}, u32[]{:S(2)}) copy-start(f32[4,128]{1,0:T(4,128)} %param.18) | copy-start | bytes 6148
  7.2 119.4 %reduce-scatter.2.cloned.1.call-start = ((), (), s32[]{:S(2)}) async-start(), calls=%async_computation.4 | async-start | bytes 36864 | tf_op jit(solution)/shard_map/reduce_scatter | solution.py:102
  75.3 20.6 %copy-start.10 = (s32[1,32,4]{1,2,0:T(4,128)S(1)}, s32[1,32,4]{1,2,0:T(4,128)}, u32[]{:S(2)}) copy-start(s32[1,32,4]{1,2,0:T(4,128)} %param.21) | copy-start | bytes 1540
  75.3 26.2 %copy-start.3 = (f32[4,3,128]{2,0,1:T(4,128)S(1)}, f32[4,3,128]{2,0,1:T(4,128)}, u32[]{:S(2)}) copy-start(f32[4,3,128]{2,0,1:T(4,128)} %param.14) | copy-start | bytes 18436
  75.3 27.1 %copy-start.4 = (f32[4,3,128]{2,0,1:T(4,128)S(1)}, f32[4,3,128]{2,0,1:T(4,128)}, u32[]{:S(2)}) copy-start(f32[4,3,128]{2,0,1:T(4,128)} %param.15) | copy-start | bytes 18436
  75.3 28.0 %copy-start.5 = (f32[4,3,128]{2,0,1:T(4,128)S(1)}, f32[4,3,128]{2,0,1:T(4,128)}, u32[]{:S(2)}) copy-start(f32[4,3,128]{2,0,1:T(4,128)} %param.16) | copy-start | bytes 18436
  75.3 28.8 %copy-start.6 = (f32[4,3,128]{2,0,1:T(4,128)S(1)}, f32[4,3,128]{2,0,1:T(4,128)}, u32[]{:S(2)}) copy-start(f32[4,3,128]{2,0,1:T(4,128)} %param.17) | copy-start | bytes 18436
  75.3 53.3 %copy-start.9 = (s32[1,32,4]{1,2,0:T(4,128)S(1)}, s32[1,32,4]{1,2,0:T(4,128)}, u32[]{:S(2)}) copy-start(s32[1,32,4]{1,2,0:T(4,128)} %param.20) | copy-start | bytes 1540
  75.3 60.0 %copy-start = (f32[128,3,128]{2,0,1:T(8,128)S(1)}, f32[128,3,128]{2,0,1:T(8,128)}, u32[]{:S(2)}) copy-start(f32[128,3,128]{2,0,1:T(8,128)} %param.22) | copy-start | bytes 589828
  75.3 60.1 %copy-start.1 = (f32[128,128]{1,0:T(8,128)S(1)}, f32[128,128]{1,0:T(8,128)}, u32[]{:S(2)}) copy-start(f32[128,128]{1,0:T(8,128)} %param.23) | copy-start | bytes 196612
  95.2 0.6 copy-start.2
  96.6 33.2 %all-to-all-start = ((s32[32,1,4]{2,1,0:T(1,128)}), s32[32,1,4]{2,1,0:T(1,128)S(1)}, u32[]{:S(2)}, u32[]{:S(2)}) async-start(s32[32,1,4]{2,1,0:T(1,128)} %copy.177), calls=%async_computation.1 | async-start | bytes 32768 | tf_op jit(solution)/shard_map/all_to_all | solution.py:139
  128.6 17.0 %copy-start.7 = (f32[3,4,128]{2,1,0:T(4,128)}, f32[3,4,128]{2,1,0:T(4,128)S(1)}, u32[]{:S(2)}) copy-start(f32[3,4,128]{2,1,0:T(4,128)S(1)} %copy.173) | copy-start | bytes 18436
  129.8 15.7 %all-to-all-start.1 = ((f32[32,4,4,128]{3,2,1,0:T(4,128)}), f32[32,4,4,128]{3,2,1,0:T(4,128)S(1)}, u32[]{:S(2)}, u32[]{:S(2)}) async-start(f32[32,4,4,128]{3,2,1,0:T(4,128)} %copy.180), calls=%async_computation.2 | async-start | bytes 524288 | tf_op jit(solution)/shard_map/all_to_all | solution.py:138
  175.0 12.2 %all-to-all-start.2 = ((f32[32,4,3,128]{3,1,2,0:T(4,128)}), f32[32,4,3,128]{3,1,2,0:T(4,128)S(1)}, u32[]{:S(2)}, u32[]{:S(2)}) async-start(f32[32,4,3,128]{3,1,2,0:T(4,128)} %copy.184), calls=%async_computation.3 | async-start | bytes 393216 | tf_op jit(solution)/shard_map/all_to_all | solution.py:161
Sparse Core Ops, SparseCore 0:
  96.0 30.5 reduce-scatter.1
where the time goes:
time: 196 us; the launch traced here: 195 us
  blocking collectives  64.2 us (33%)
  other arithmetic  49.9 us (25%)
  waiting for transfers between devices  36.7 us (19%)
  between operations  14.3 us (7%)
  local copies, waits for them, and re-layouts  13.3 us (7%)
  starting transfers between devices  13.2 us (7%)
  matrix products  2.45 us (1%)
    reduce_scatter x1, waiting for transfers between devices, local(): forces = lax.psum_scatter(terms, 'col', scatter_dimension=1, tiled=True)  21.6 us
    all_gather x1, blocking collectives, local(): lax.all_gather(pos_flat, 'row', axis=1, tiled=True)  21 us
    all_gather x1, blocking collectives, local(): lax.all_gather(vel_flat, 'row', axis=1, tiled=True)  19.4 us
    reduce_sum x8, other arithmetic, entry_one(): kick = jnp.sum(delta * (gmass[:, None, :] * cube)[:, None], -1)  15.6 us
    all_gather x1, blocking collectives, local(): lax.all_gather(active, 'col', axis=1, tiled=True)  14.5 us
    all_gather x1, blocking collectives, local(): lax.all_gather(mass_flat, 'row', axis=0, tiled=True)  9.28 us
    reduce_sum x2, other arithmetic, pair_block(): accel = jnp.sum(delta * weight[None], -1)  8.6 us
    all_to_all x1, waiting for transfers between devices, local(): lax.all_to_all(outgoing, ('row', 'col'), split_axis=0, concat_axis=0, til...  8.39 us
  transfers between devices with their start and end apart: 4, of which 3 were waited for; matrix products, arithmetic and copies ran while one was open for 6% of the time, Pallas kernels for 0%

commit v1 on v0

v1 whole, which is shorter than its diff:
```python
import functools

import jax
import jax.numpy as jnp
from jax import lax
from jax.experimental import pallas as pl
from jax.experimental.pallas import tpu as pltpu
from jax.sharding import PartitionSpec as P

MESH = pl.DeviceIdType.MESH
step_length = 1.0
half = 0.5 * step_length**2
sixth = step_length**3 / 6.0
twelfth = step_length**2 / 12.0
soft_star = 0.01
soft_galaxy = 0.04
F32 = jnp.float32
BF16 = jnp.bfloat16


def row_of(x):
    return lax.broadcasted_iota(jnp.int32, x.shape, 0)


def swap(x):
    return pltpu.roll(x, 4, 0)


def rounded(x):
    return x.astype(BF16).astype(F32)


def split3(x):
    high = rounded(x)
    rest = x - high
    mid = rounded(rest)
    return high, mid, rest - mid


def split2(x):
    high = rounded(x)
    return high, x - high


def predict(a, b):
    pos = a + step_length * swap(a) + half * b + sixth * swap(b)
    vel = a + step_length * swap(b) + half * b
    return jnp.where(row_of(a) < 4, pos, vel)


def stack_left(table):
    high, mid, low = split3(table)
    ones = jnp.where(row_of(table) < 3, 1.0, 0.0)
    return jnp.concatenate([high, high, high, mid, mid, low, ones, jnp.zeros_like(table)], 0)


def stack_right(table, const):
    high, mid, low = split3(table)
    ch, cm, cl = split3(const)
    row = row_of(table)
    last = jnp.where(row == 0, ch, jnp.where(row == 1, cm, jnp.where(row == 2, cl, 0.0)))
    return jnp.concatenate(
        [high, mid, low, high, mid, high, last, jnp.zeros_like(table)], 0
    ).astype(BF16)


def sum3(x):
    return jnp.sum(jnp.where(row_of(x) < 3, x, 0.0), 0, keepdims=True)


def dot(a, b):
    return lax.dot_general(a, b, (((1,), (0,)), ((), ())), preferred_element_type=F32)


def dot_t(a, b):
    return lax.dot_general(a, b, (((1,), (1,)), ((), ())), preferred_element_type=F32)


def cube_parts(x):
    high = x.astype(BF16)
    return high, (x - high.astype(F32)).astype(BF16)


def kernel(
    rows,
    cols,
    spos,
    svel,
    sacc,
    sjerk,
    smass,
    index,
    sblock,
    lists,
    gpos,
    gmass,
    out_pos,
    out_vel,
    pulls,
    lists_in,
    base_a,
    base_b,
    onehot,
    act_all,
    star_all,
    left,
    right2,
    rightd,
    weigh,
    acc_u,
    acc_q,
    part_out,
    part_in,
    leaves_out,
    leaves_in,
    pull_out,
    sleft,
    sfeat,
    fresh,
    lists_s,
    list_send,
    list_recv,
    act_send,
    act_recv,
    star_send,
    star_recv,
    leaf_send,
    leaf_recv,
    part_send,
    part_recv,
    pull_send,
    pull_recv,
    local_sem,
):
    mr = lax.axis_index("row")
    mc = lax.axis_index("col")
    count = rows * cols
    me = mr * cols + mc
    nblock, _, width = spos.shape
    slots = sblock.shape[2]
    stars = nblock * width
    nact = index.shape[1]

    def where_is(flat):
        return (flat // cols, flat % cols)

    barrier = pltpu.get_barrier_semaphore()

    def greet(off, carry):
        pl.semaphore_signal(
            barrier, inc=1, device_id=where_is((me + off) % count), device_id_type=MESH
        )
        return carry

    lax.fori_loop(1, count, greet, 0)

    base_a[...] = jnp.zeros_like(base_a)
    base_b[...] = jnp.zeros_like(base_b)
    for b in range(nblock):
        at = pl.ds(b * width, width)
        base_a[0:3, at] = spos[b]
        base_a[4:7, at] = svel[b]
        base_b[0:3, at] = sacc[b]
        base_b[4:7, at] = sjerk[b]
    ta = base_a[...]
    tb = base_b[...]
    pred = predict(ta, tb)
    base_a[...] = pred
    for b in range(nblock):
        at = pl.ds(b * width, width)
        base_a[3:4, at] = smass[b : b + 1, :]
    star_all[mr] = base_a[...]
    hot = lax.broadcasted_iota(jnp.int32, (stars, nact), 0) == index[...]
    onehot[...] = hot.astype(F32).astype(BF16)
    parts = jnp.concatenate(split3(ta) + split3(tb), 0).astype(BF16)
    got = dot(parts, onehot[...])
    sel_a = got[0:8] + got[8:16] + got[16:24]
    sel_b = got[24:32] + got[32:40] + got[40:48]
    mine = predict(sel_a, sel_b)
    row8 = row_of(mine)
    mine = jnp.where(
        row8 == 3, sum3(mine * mine), jnp.where(row8 == 7, sum3(mine * swap(mine)), mine)
    )
    act_all[mc] = mine

    pl.semaphore_wait(barrier, count - 1)

    def act_copy(peer, slot):
        return pltpu.make_async_remote_copy(
            src_ref=act_all.at[mc],
            dst_ref=act_all.at[mc],
            send_sem=act_send.at[peer],
            recv_sem=act_recv.at[slot],
            device_id=(mr, peer),
            device_id_type=MESH,
        )

    def star_copy(peer, slot):
        return pltpu.make_async_remote_copy(
            src_ref=star_all.at[mr],
            dst_ref=star_all.at[mr],
            send_sem=star_send.at[peer],
            recv_sem=star_recv.at[slot],
            device_id=(peer, mc),
            device_id_type=MESH,
        )

    def list_copy(peer, slot):
        return pltpu.make_async_remote_copy(
            src_ref=lists.at[peer],
            dst_ref=lists_in.at[me],
            send_sem=list_send.at[peer],
            recv_sem=list_recv.at[slot],
            device_id=where_is(peer),
            device_id_type=MESH,
        )

    def leaf_copy(peer, slot):
        return pltpu.make_async_remote_copy(
            src_ref=leaves_out.at[peer],
            dst_ref=leaves_in.at[me],
            send_sem=leaf_send.at[peer],
            recv_sem=leaf_recv.at[slot],
            device_id=where_is(peer),
            device_id_type=MESH,
        )

    def part_copy(peer, slot):
        return pltpu.make_async_remote_copy(
            src_ref=part_out.at[peer],
            dst_ref=part_in.at[mc],
            send_sem=part_send.at[peer],
            recv_sem=part_recv.at[slot],
            device_id=(mr, peer),
            device_id_type=MESH,
        )

    def pull_copy(peer, slot):
        return pltpu.make_async_remote_copy(
            src_ref=pull_out.at[peer],
            dst_ref=pulls.at[me],
            send_sem=pull_send.at[peer],
            recv_sem=pull_recv.at[slot],
            device_id=where_is(peer),
            device_id_type=MESH,
        )

    def each(size, here, act):
        def body(off, carry):
            act((here + off) % size)
            return carry

        lax.fori_loop(1, size, body, 0)

    each(cols, mc, lambda peer: act_copy(peer, mc).start())
    each(rows, mr, lambda peer: star_copy(peer, mr).start())
    each(count, me, lambda peer: list_copy(peer, me).start())
    lists_in[me] = lists[me]

    def prepare(r):
        table = star_all[r]
        row = row_of(table)
        body = (row != 3) & (row != 7)
        mass = table[3:4]
        right2[...] = stack_right(
            jnp.where(row < 3, -2.0 * table, jnp.where(row == 3, 1.0, 0.0)),
            sum3(table * table) + soft_star,
        )
        turned = swap(table)
        rightd[...] = stack_right(
            jnp.where(body, -turned, jnp.where(row == 7, 1.0, 0.0)), sum3(table * turned)
        )
        high, low = split2(jnp.where(body, table * mass, jnp.where(row == 3, mass, 0.0)))
        pad = jnp.zeros((weigh.shape[0] - 16, stars), F32)
        weigh[...] = jnp.concatenate([high, low, pad], 0).astype(BF16)

    def pairs(c):
        lhs = left[c]
        r2 = dot(lhs, right2[...])
        along = dot(lhs, rightd[...])
        inv = lax.rsqrt(r2)
        inv2 = inv * inv
        u = inv2 * inv
        q = u * inv2 * along
        uh, ul = cube_parts(u)
        qh, ql = cube_parts(q)
        w = weigh[...]
        acc_u[c] += dot_t(uh, w) + dot_t(ul, w)
        acc_q[c] += dot_t(qh, w) + dot_t(ql, w)

    def left_of(c):
        left[c] = stack_left(act_all[c]).T.astype(BF16)

    acc_u[...] = jnp.zeros_like(acc_u)
    acc_q[...] = jnp.zeros_like(acc_q)
    prepare(mr)
    left_of(mc)
    pairs(mc)

    def take_active(off, carry):
        c = (mc + off) % cols
        act_copy(c, c).wait_recv()
        left_of(c)
        pairs(c)
        return carry

    lax.fori_loop(1, cols, take_active, 0)

    each(count, me, lambda peer: list_copy(peer, peer).wait_recv())
    move = pltpu.make_async_copy(lists_in, lists_s, local_sem)
    move.start()
    move.wait()

    def grab(peer, ref):
        for s in range(slots):
            leaf = lists_s[peer, 0, s]
            live = leaf >= 0
            at = jnp.maximum(leaf, 0)
            keep = jnp.where(live, 1.0, 0.0)
            ref[peer, 4 * s : 4 * s + 3, :] = gpos[at] * keep
            ref[peer, 4 * s + 3 : 4 * s + 4, :] = gmass[pl.ds(at, 1), :] * keep

    grab(me, leaves_in)

    def serve(peer):
        grab(peer, leaves_out)
        leaf_copy(peer, me).start()

    each(count, me, serve)

    def take_stars(off, carry):
        r = (mr + off) % rows
        star_copy(r, r).wait_recv()
        prepare(r)

        def inner(c, carry):
            pairs(c)
            return carry

        lax.fori_loop(0, cols, inner, 0)
        return carry

    lax.fori_loop(1, rows, take_stars, 0)

    def finish(c):
        su = acc_u[c].T
        sq = acc_q[c].T
        su = su[0:8] + su[8:16]
        sq = sq[0:8] + sq[8:16]
        table = act_all[c]
        su = su - table * su[3:4]
        sq = sq - table * sq[3:4]
        return jnp.where(row8 < 4, su, su - 3.0 * swap(sq))

    def give(c):
        part_out[c] = finish(c)
        part_copy(c, mc).start()

    each(cols, mc, give)
    total = finish(mc)

    def collect(off, total):
        c = (mc + off) % cols
        part_copy(c, c).wait_recv()
        return total + part_in[c]

    total = lax.fori_loop(1, cols, collect, total)

    gap = (sel_b - total) * twelfth
    vel_one = sel_a + swap(sel_b + total) * (0.5 * step_length) + gap
    pos_one = sel_a + swap(sel_a + vel_one) * (0.5 * step_length) + gap
    new = jnp.where(row8 < 4, pos_one, vel_one)
    new = jnp.where(row8 == 3, 1.0, jnp.where(row8 == 7, 0.0, new))
    parts = jnp.concatenate(split3(new) + (jnp.zeros_like(new),), 0).astype(BF16)
    spread = dot_t(parts, onehot[...])
    spread = spread[0:8] + spread[8:16] + spread[16:24]
    fresh[...] = jnp.where(spread[3:4] > 0.5, spread, base_a[...])

    for b in range(nblock):
        at = pl.ds(b * width, width)
        table = fresh[:, at]
        mass = smass[b : b + 1, :]
        out_pos[b] = table[0:3]
        only = jnp.where(row8 < 3, table, 0.0)
        only = jnp.where(row8 == 3, sum3(only * only), only)
        sleft[b] = stack_left(only).T.astype(BF16)
        high, low = split2(jnp.where(row8 < 3, table * mass, jnp.where(row8 == 3, mass, 0.0)))
        both = jnp.concatenate([high, low], 0).astype(BF16)
        sfeat[b] = jnp.concatenate([both, both], 1)

    def entry(peer, s, kicks):
        block = sblock[0, peer, s]
        at = jnp.maximum(block, 0)
        leaf = leaves_in[peer, 4 * s : 4 * s + 4, :]
        leaf = jnp.concatenate([leaf, jnp.zeros_like(leaf)], 0)
        row = row_of(leaf)
        mass = leaf[3:4]
        feat = stack_right(
            jnp.where(row < 3, -2.0 * leaf, jnp.where(row == 3, 1.0, 0.0)),
            sum3(leaf * leaf) + soft_galaxy,
        )
        inv = lax.rsqrt(dot(sleft[at], feat))
        uh, ul = cube_parts(inv * inv * inv)
        high, low = split2(jnp.where(row < 3, leaf * mass, jnp.where(row == 3, mass, 0.0)))
        both = jnp.concatenate([high, low], 0).astype(BF16)
        kick = dot_t(both, uh) + dot_t(both, ul)
        kick = kick[0:8] + kick[8:16]
        pull = dot(sfeat[at], jnp.concatenate([uh, ul], 0))
        pull = pull[0:8] + pull[8:16]
        pull = pull - leaf * pull[3:4]
        return pull[0:3], tuple(
            k + jnp.where(block == b, kick, 0.0) for b, k in enumerate(kicks)
        )

    def entries(peer, ref, kicks):
        for s in range(slots):
            pull, kicks = entry(peer, s, kicks)
            ref[peer, 3 * s : 3 * s + 3, :] = pull
        return kicks

    def work(off, kicks):
        peer = (me + off) % count
        leaf_copy(peer, peer).wait_recv()
        kicks = entries(peer, pull_out, kicks)
        pull_copy(peer, me).start()
        return kicks

    kicks = tuple(jnp.zeros((8, width), F32) for _ in range(nblock))
    kicks = lax.fori_loop(1, count, work, kicks)
    kicks = entries(me, pulls, kicks)
    for b in range(nblock):
        table = fresh[:, pl.ds(b * width, width)]
        kick = kicks[b] - table * kicks[b][3:4]
        out_vel[b] = table[4:7] + step_length * kick[0:3]

    each(count, me, lambda peer: pull_copy(peer, peer).wait_recv())
    each(cols, mc, lambda peer: act_copy(peer, mc).wait_send())
    each(rows, mr, lambda peer: star_copy(peer, mr).wait_send())
    each(cols, mc, lambda peer: part_copy(peer, mc).wait_send())

    def drain(peer):
        list_copy(peer, me).wait_send()
        leaf_copy(peer, me).wait_send()
        pull_copy(peer, me).wait_send()

    each(count, me, drain)


def gather_kernel(scale, pulls, lists, pos, vel, out, out_pos, out_vel):
    count = pulls.shape[0]
    slots = pulls.shape[1] // 3
    out[...] = jnp.zeros_like(out)
    out_pos[...] = pos[...]
    out_vel[...] = vel[...]

    def body(source, carry):
        for s in range(slots):
            leaf = lists[source, 0, s]

            @pl.when(leaf >= 0)
            def add():
                out[leaf] += pulls[source, 3 * s : 3 * s + 3, :] * scale

        return carry

    lax.fori_loop(0, count, body, 0)


def local(
    rows,
    cols,
    star_pos,
    star_vel,
    star_acc,
    star_jerk,
    star_mass,
    active_index,
    send_block,
    send_leaf,
    galaxy_pos,
    galaxy_mass,
):
    count = rows * cols
    nblock, _, width = star_pos.shape
    stars = nblock * width
    nact = active_index.shape[1]
    slots = send_leaf.shape[2]
    depth = galaxy_pos.shape[2]
    lists = jnp.pad(send_leaf[0][:, None, :], ((0, 0), (0, 0), (0, 128 - slots)))
    vmem = pl.BlockSpec(memory_space=pltpu.VMEM)
    smem = pl.BlockSpec(memory_space=pltpu.SMEM)
    dma = pltpu.SemaphoreType.DMA
    pos, vel, pulls, arrived = pl.pallas_call(
        functools.partial(kernel, rows, cols),
        out_shape=(
            jax.ShapeDtypeStruct(star_pos.shape, F32),
            jax.ShapeDtypeStruct(star_vel.shape, F32),
            jax.ShapeDtypeStruct((count, 3 * slots, depth), F32),
            jax.ShapeDtypeStruct((count, 1, 128), jnp.int32),
        ),
        in_specs=[vmem] * 6 + [smem] + [vmem] * 3,
        out_specs=(vmem,) * 4,
        scratch_shapes=[
            pltpu.VMEM((8, stars), F32),
            pltpu.VMEM((8, stars), F32),
            pltpu.VMEM((stars, nact), BF16),
            pltpu.VMEM((cols, 8, nact), F32),
            pltpu.VMEM((rows, 8, stars), F32),
            pltpu.VMEM((cols, nact, 64), BF16),
            pltpu.VMEM((64, stars), BF16),
            pltpu.VMEM((64, stars), BF16),
            pltpu.VMEM((128, stars), BF16),
            pltpu.VMEM((cols, nact, 128), F32),
            pltpu.VMEM((cols, nact, 128), F32),
            pltpu.VMEM((cols, 8, nact), F32),
            pltpu.VMEM((cols, 8, nact), F32),
            pltpu.VMEM((count, 4 * slots, depth), F32),
            pltpu.VMEM((count, 4 * slots, depth), F32),
            pltpu.VMEM((count, 3 * slots, depth), F32),
            pltpu.VMEM((nblock, width, 64), BF16),
            pltpu.VMEM((nblock, 16, 2 * width), BF16),
            pltpu.VMEM((8, stars), F32),
            pltpu.SMEM((count, 1, 128), jnp.int32),
            dma((count,)),
            dma((count,)),
            dma((cols,)),
            dma((cols,)),
            dma((rows,)),
            dma((rows,)),
            dma((count,)),
            dma((count,)),
            dma((cols,)),
            dma((cols,)),
            dma((count,)),
            dma((count,)),
            dma(()),
        ],
        compiler_params=pltpu.CompilerParams(
            collective_id=0, has_side_effects=True, vmem_limit_bytes=48 * 1024 * 1024
        ),
    )(
        star_pos,
        star_vel,
        star_acc,
        star_jerk,
        star_mass,
        active_index,
        send_block,
        lists,
        galaxy_pos,
        galaxy_mass,
    )
    accel, pos, vel = pl.pallas_call(
        functools.partial(gather_kernel, float(nblock * count)),
        out_shape=(
            jax.ShapeDtypeStruct(galaxy_pos.shape, F32),
            jax.ShapeDtypeStruct(star_pos.shape, F32),
            jax.ShapeDtypeStruct(star_vel.shape, F32),
        ),
        in_specs=[vmem, smem, vmem, vmem],
        out_specs=(vmem,) * 3,
        compiler_params=pltpu.CompilerParams(vmem_limit_bytes=48 * 1024 * 1024),
    )(pulls, arrived, pos, vel)
    return (pos, vel, accel)


def solution(mesh):
    rows = mesh.shape["row"]
    cols = mesh.shape["col"]
    three = P(("row", "col"), None, None)
    two = P(("row", "col"), None)
    return jax.shard_map(
        functools.partial(local, rows, cols),
        mesh=mesh,
        in_specs=(three, three, three, three, two, two, three, three, three, two),
        out_specs=(three, three, three),
        check_vma=False,
    )
```

time: 196 us -> 69.5 us (0.35)
  blocking collectives: 64.2 us -> 0 us
  Pallas kernels: 0 us -> 61.9 us
  other arithmetic: 49.9 us -> 0 us
  waiting for transfers between devices: 36.7 us -> 0 us
  between operations: 14.3 us -> 0.72 us
  starting transfers between devices: 13.2 us -> 0 us
  local copies, waits for them, and re-layouts: 13.3 us -> 6.54 us
  matrix products: 2.45 us -> 0 us
    all_gather x4 -> x0, blocking collectives: 64.2 us -> none  [the longest x1 21 us: local(): lax.all_gather(pos_flat, 'row', axis=1, tiled=True)]
    pallas_call x0 -> x2, Pallas kernels: none -> 61.9 us  [the longest x1 59.7 us: local(): pl.pallas_call(functools.partial(kernel, rows, cols), out_shape=(jax.Shap...]
    reduce_sum x20 -> x0, other arithmetic: 39.8 us -> none  [the longest x8 15.6 us: entry_one(): kick = jnp.sum(delta * (gmass[:, None, :] * cube)[:, None], -1)]
    reduce_scatter x1 -> x0, waiting for transfers between devices: 21.6 us -> none  [local(): forces = lax.psum_scatter(terms, 'col', scatter_dimension=1, tiled=True)]
    all_to_all x3 -> x0, waiting for transfers between devices: 15.1 us -> none  [the longest x1 8.39 us: local(): lax.all_to_all(outgoing, ('row', 'col'), split_axis=0, concat_axis=0, til...]
    all_to_all x3 -> x0, starting transfers between devices: 13.1 us -> none  [the longest x1 5.48 us: local(): lax.all_to_all(outgoing, ('row', 'col'), split_axis=0, concat_axis=0, til...]
    mul x10 -> x0, other arithmetic: 6.99 us -> none  [the longest x2 3.86 us: pair_block(): jerks = jnp.sum((dvel - 3.0 * along[None] * delta) * weight[None], -1)]
    unnamed x27 -> x25, local copies, waits for them, and re-layouts: 1.01 us -> 6.44 us
  transfers between devices with their start and end apart: 4 -> 0, of which waited for: 3 -> 0; matrix products, arithmetic and copies ran while one was open for 6% -> 0% of each run, Pallas kernels for 0% -> 0%
where the time goes in v1:
time: 69.5 us; the launch traced here: 69.2 us
  Pallas kernels  61.9 us (89%)
  local copies, waits for them, and re-layouts  6.54 us (9%)
  between operations  0.72 us (1%)
    pallas_call x1, Pallas kernels, local(): pl.pallas_call(functools.partial(kernel, rows, cols), out_shape=(jax.Shap...  59.7 us
    unnamed x25, local copies, waits for them, and re-layouts  6.44 us
    pallas_call x1, Pallas kernels, local(): pl.pallas_call(functools.partial(gather_kernel, float(nblock * count)), o...  2.18 us

profile of v1, /device:TPU:1, one launch (start us, length us, event | category | flops | bytes accessed | tf_op | source)
XLA Modules:
  0.0 69.2 jit_solution(3213251088389667347)
XLA Ops:
  0.6 0.0 copy-start.3
  0.6 0.7 %copy.14.spos = f32[4,3,128]{2,1,0:T(4,128)S(1)} copy(f32[4,3,128]{2,0,1:T(4,128)} %param.10) | data formatting | bytes 12288 | tf_op args[0]
  1.3 0.0 copy-done.3
  1.3 0.0 copy-start.4
  1.4 0.7 copy-done.4
  2.0 0.0 copy-start.5
  2.0 0.7 copy-done.5
  2.7 0.0 copy-start.6
  2.7 0.7 copy-done.6
  3.4 0.0 copy-start.7
  3.4 0.1 copy.18.sblock
  3.5 0.6 copy-done.7
  4.1 0.1 copy.13
  4.2 0.0 copy-start
  4.2 0.0 copy-start.1
  4.2 0.0 copy-start.2
  4.2 1.1 %copy.19.gpos = f32[128,3,128]{2,1,0:T(4,128)S(1)} copy(f32[128,3,128]{2,0,1:T(8,128)} %param.18) | data formatting | bytes 393216 | tf_op args[8]
  5.3 0.0 copy-done
  5.3 0.0 copy-done.1
  5.3 0.0 copy-done.2
  5.4 59.7 %shard_map.121 = (f32[4,3,128]{2,1,0:T(4,128)S(1)}, f32[4,3,128]{2,1,0:T(4,128)S(1)}, f32[32,12,128]{2,1,0:T(8,128)S(1)}, s32[32,1,128]{2,1,0:T(1,128)S(1)}) custom-call(f32[4,3,128]{2,1,0:T(4,128)S(1)} %copy.14.spos, f32[4,3,128]{2,1,0:T(4,128)S(1)} %copy.15.svel, f32[4,3,128]{2,1,0:T(4,128)S(1)} %copy.16.sacc, f32[4,3,128]{2,1,0:T(4,128)S(1)} %copy.17.sjerk, ...), custom_call_target="tpu_custom_call" | custom-call | tf_op jit(solution)/shard_map/pallas_call | solution.py:493
  65.1 2.2 %shard_map.122 = (f32[128,3,128]{2,1,0:T(4,128)S(1)}, f32[4,3,128]{2,1,0:T(4,128)S(1)}, f32[4,3,128]{2,1,0:T(4,128)S(1)}) custom-call(f32[32,12,128]{2,1,0:T(8,128)S(1)} %get-tuple-element.10.pulls, s32[32,1,128]{2,1,0:T(1,128)S(1)} %get-tuple-element.11.lists, f32[4,3,128]{2,1,0:T(4,128)S(1)} %get-tuple-element.12.pos, f32[4,3,128]{2,1,0:T(4,128)S(1)} %get-tuple-element.13.vel), custom_call_target="tpu_custom_call" | custom-call | tf_op jit(solution)/shard_map/pallas_call | solution.py:553
  67.3 0.6 copy.20
  67.9 0.6 copy.21
  68.5 0.7 copy.22
  (4 shorter events, 0.0 us)
Async XLA Ops:
  0.6 0.7 %copy-start.3 = (f32[4,3,128]{2,0,1:T(4,128)S(1)}, f32[4,3,128]{2,0,1:T(4,128)}, u32[]{:S(2)}) copy-start(f32[4,3,128]{2,0,1:T(4,128)} %param.11) | copy-start | bytes 18436
  1.3 0.7 %copy-start.4 = (f32[4,3,128]{2,0,1:T(4,128)S(1)}, f32[4,3,128]{2,0,1:T(4,128)}, u32[]{:S(2)}) copy-start(f32[4,3,128]{2,0,1:T(4,128)} %param.12) | copy-start | bytes 18436
  2.0 0.7 %copy-start.5 = (f32[4,3,128]{2,0,1:T(4,128)S(1)}, f32[4,3,128]{2,0,1:T(4,128)}, u32[]{:S(2)}) copy-start(f32[4,3,128]{2,0,1:T(4,128)} %param.13) | copy-start | bytes 18436
  2.7 0.7 copy-start.6
  3.4 0.7 copy-start.7
  4.2 1.1 %copy-start = (f32[128,128]{1,0:T(8,128)S(1)}, f32[128,128]{1,0:T(8,128)}, u32[]{:S(2)}) copy-start(f32[128,128]{1,0:T(8,128)} %gmass.1) | copy-start | bytes 196612
  4.2 1.1 %copy-start.1 = (f32[4,128]{1,0:T(4,128)S(1)}, f32[4,128]{1,0:T(4,128)}, u32[]{:S(2)}) copy-start(f32[4,128]{1,0:T(4,128)} %smass.1) | copy-start | bytes 6148
  4.2 1.1 %copy-start.2 = (s32[1,128]{1,0:T(1,128)S(1)}, s32[1,128]{1,0:T(1,128)}, u32[]{:S(2)}) copy-start(s32[1,128]{1,0:T(1,128)} %index.1) | copy-start | bytes 1540

commit v2 on v1

--- a/solution.py
+++ b/solution.py
@@ -96,8 +96,7 @@
     gmass,
     out_pos,
     out_vel,
-    pulls,
-    lists_in,
+    out_accel,
     base_a,
     base_b,
     onehot,
@@ -114,9 +113,14 @@
     leaves_out,
     leaves_in,
     pull_out,
+    pulls,
+    keys,
+    pick,
+    kicks,
     sleft,
     sfeat,
     fresh,
+    lists_in,
     lists_s,
     list_send,
     list_recv,
@@ -136,8 +140,8 @@
     mc = lax.axis_index("col")
     count = rows * cols
     me = mr * cols + mc
-    nblock, _, width = spos.shape
-    slots = sblock.shape[2]
+    _, nblock, width = spos.shape
+    slots = sblock.shape[0]
     stars = nblock * width
     nact = index.shape[1]
 
@@ -158,10 +162,10 @@
     base_b[...] = jnp.zeros_like(base_b)
     for b in range(nblock):
         at = pl.ds(b * width, width)
-        base_a[0:3, at] = spos[b]
-        base_a[4:7, at] = svel[b]
-        base_b[0:3, at] = sacc[b]
-        base_b[4:7, at] = sjerk[b]
+        base_a[0:3, at] = spos[:, b, :]
+        base_a[4:7, at] = svel[:, b, :]
+        base_b[0:3, at] = sacc[:, b, :]
+        base_b[4:7, at] = sjerk[:, b, :]
     ta = base_a[...]
     tb = base_b[...]
     pred = predict(ta, tb)
@@ -271,8 +275,8 @@
             jnp.where(body, -turned, jnp.where(row == 7, 1.0, 0.0)), sum3(table * turned)
         )
         high, low = split2(jnp.where(body, table * mass, jnp.where(row == 3, mass, 0.0)))
-        pad = jnp.zeros((weigh.shape[0] - 16, stars), F32)
-        weigh[...] = jnp.concatenate([high, low, pad], 0).astype(BF16)
+        pad = jnp.zeros((weigh.shape[1] - 16, stars), F32)
+        weigh[...] = jnp.concatenate([high, low, pad], 0).T.astype(BF16)
 
     def pairs(c):
         lhs = left[c]
@@ -285,8 +289,8 @@
         uh, ul = cube_parts(u)
         qh, ql = cube_parts(q)
         w = weigh[...]
-        acc_u[c] += dot_t(uh, w) + dot_t(ul, w)
-        acc_q[c] += dot_t(qh, w) + dot_t(ql, w)
+        acc_u[c] += dot(uh, w) + dot(ul, w)
+        acc_q[c] += dot(qh, w) + dot(ql, w)
 
     def left_of(c):
         left[c] = stack_left(act_all[c]).T.astype(BF16)
@@ -317,8 +321,10 @@
             live = leaf >= 0
             at = jnp.maximum(leaf, 0)
             keep = jnp.where(live, 1.0, 0.0)
-            ref[peer, 4 * s : 4 * s + 3, :] = gpos[at] * keep
+            for c in range(3):
+                ref[peer, 4 * s + c : 4 * s + c + 1, :] = gpos[c, pl.ds(at, 1), :] * keep
             ref[peer, 4 * s + 3 : 4 * s + 4, :] = gmass[pl.ds(at, 1), :] * keep
+            keys[peer, 4 * s : 4 * s + 4, :] = jnp.full((4, width), leaf, jnp.int32)
 
     grab(me, leaves_in)
 
@@ -327,6 +333,13 @@
         leaf_copy(peer, me).start()
 
     each(count, me, serve)
+
+    key = keys[...].reshape(count * 4 * slots, width)
+    component = row_of(key) % 4
+    lane = lax.broadcasted_iota(jnp.int32, key.shape, 1)
+    for c in range(3):
+        match = jnp.where((key == lane) & (component == c), 1.0, 0.0)
+        pick[c * width : (c + 1) * width, :] = match.T.astype(BF16)
 
     def take_stars(off, carry):
         r = (mr + off) % rows
@@ -380,7 +393,7 @@
         at = pl.ds(b * width, width)
         table = fresh[:, at]
         mass = smass[b : b + 1, :]
-        out_pos[b] = table[0:3]
+        out_pos[:, b, :] = table[0:3]
         only = jnp.where(row8 < 3, table, 0.0)
         only = jnp.where(row8 == 3, sum3(only * only), only)
         sleft[b] = stack_left(only).T.astype(BF16)
@@ -388,50 +401,51 @@
         both = jnp.concatenate([high, low], 0).astype(BF16)
         sfeat[b] = jnp.concatenate([both, both], 1)
 
-    def entry(peer, s, kicks):
-        block = sblock[0, peer, s]
-        at = jnp.maximum(block, 0)
-        leaf = leaves_in[peer, 4 * s : 4 * s + 4, :]
-        leaf = jnp.concatenate([leaf, jnp.zeros_like(leaf)], 0)
-        row = row_of(leaf)
-        mass = leaf[3:4]
-        feat = stack_right(
-            jnp.where(row < 3, -2.0 * leaf, jnp.where(row == 3, 1.0, 0.0)),
-            sum3(leaf * leaf) + soft_galaxy,
-        )
-        inv = lax.rsqrt(dot(sleft[at], feat))
-        uh, ul = cube_parts(inv * inv * inv)
-        high, low = split2(jnp.where(row < 3, leaf * mass, jnp.where(row == 3, mass, 0.0)))
-        both = jnp.concatenate([high, low], 0).astype(BF16)
-        kick = dot_t(both, uh) + dot_t(both, ul)
-        kick = kick[0:8] + kick[8:16]
-        pull = dot(sfeat[at], jnp.concatenate([uh, ul], 0))
-        pull = pull[0:8] + pull[8:16]
-        pull = pull - leaf * pull[3:4]
-        return pull[0:3], tuple(
-            k + jnp.where(block == b, kick, 0.0) for b, k in enumerate(kicks)
-        )
-
-    def entries(peer, ref, kicks):
+    def entries(peer, ref):
+        weights = []
+        feats = []
         for s in range(slots):
-            pull, kicks = entry(peer, s, kicks)
-            ref[peer, 3 * s : 3 * s + 3, :] = pull
-        return kicks
-
-    def work(off, kicks):
+            block = sblock[s, peer]
+            at = jnp.maximum(block, 0)
+            leaf = leaves_in[peer, 4 * s : 4 * s + 4, :]
+            leaf = jnp.concatenate([leaf, jnp.zeros_like(leaf)], 0)
+            row = row_of(leaf)
+            mass = leaf[3:4]
+            feat = stack_right(
+                jnp.where(row < 3, -2.0 * leaf, jnp.where(row == 3, 1.0, 0.0)),
+                sum3(leaf * leaf) + soft_galaxy,
+            )
+            inv = lax.rsqrt(dot(sleft[at], feat))
+            uh, ul = cube_parts(inv * inv * inv)
+            high, low = split2(jnp.where(row < 3, leaf * mass, jnp.where(row == 3, mass, 0.0)))
+            both = jnp.concatenate([high, low], 0)
+            both = jnp.concatenate(
+                [both * jnp.where(block == b, 1.0, 0.0) for b in range(nblock)], 0
+            ).astype(BF16)
+            weights += [uh, ul]
+            feats += [both, both]
+            pull = dot(sfeat[at], jnp.concatenate([uh, ul], 0))
+            pull = pull[0:8] + pull[8:16]
+            pull = pull - leaf * pull[3:4]
+            ref[peer, 4 * s : 4 * s + 4, :] = pull[0:4]
+        kicks[...] += dot_t(jnp.concatenate(weights, 1), jnp.concatenate(feats, 1))
+
+    def work(off, carry):
         peer = (me + off) % count
         leaf_copy(peer, peer).wait_recv()
-        kicks = entries(peer, pull_out, kicks)
+        entries(peer, pull_out)
         pull_copy(peer, me).start()
-        return kicks
-
-    kicks = tuple(jnp.zeros((8, width), F32) for _ in range(nblock))
-    kicks = lax.fori_loop(1, count, work, kicks)
-    kicks = entries(me, pulls, kicks)
+        return carry
+
+    kicks[...] = jnp.zeros_like(kicks)
+    lax.fori_loop(1, count, work, 0)
+    entries(me, pulls)
+    turned = kicks[...].T
     for b in range(nblock):
         table = fresh[:, pl.ds(b * width, width)]
-        kick = kicks[b] - table * kicks[b][3:4]
-        out_vel[b] = table[4:7] + step_length * kick[0:3]
+        kick = turned[16 * b : 16 * b + 8] + turned[16 * b + 8 : 16 * b + 16]
+        kick = kick - table * kick[3:4]
+        out_vel[:, b, :] = table[4:7] + step_length * kick[0:3]
 
     each(count, me, lambda peer: pull_copy(peer, peer).wait_recv())
     each(cols, mc, lambda peer: act_copy(peer, mc).wait_send())
@@ -445,25 +459,11 @@
 
     each(count, me, drain)
 
-
-def gather_kernel(scale, pulls, lists, pos, vel, out, out_pos, out_vel):
-    count = pulls.shape[0]
-    slots = pulls.shape[1] // 3
-    out[...] = jnp.zeros_like(out)
-    out_pos[...] = pos[...]
-    out_vel[...] = vel[...]
-
-    def body(source, carry):
-        for s in range(slots):
-            leaf = lists[source, 0, s]
-
-            @pl.when(leaf >= 0)
-            def add():
-                out[leaf] += pulls[source, 3 * s : 3 * s + 3, :] * scale
-
-        return carry
-
-    lax.fori_loop(0, count, body, 0)
+    high, low = split2(pulls[...].reshape(count * 4 * slots, width))
+    accel = dot(pick[...], high.astype(BF16)) + dot(pick[...], low.astype(BF16))
+    accel = accel * float(nblock * count)
+    for c in range(3):
+        out_accel[c] = accel[c * width : (c + 1) * width]
 
 
 def local(
@@ -485,21 +485,20 @@
     stars = nblock * width
     nact = active_index.shape[1]
     slots = send_leaf.shape[2]
-    depth = galaxy_pos.shape[2]
+    leaves, _, depth = galaxy_pos.shape
     lists = jnp.pad(send_leaf[0][:, None, :], ((0, 0), (0, 0), (0, 128 - slots)))
     vmem = pl.BlockSpec(memory_space=pltpu.VMEM)
     smem = pl.BlockSpec(memory_space=pltpu.SMEM)
     dma = pltpu.SemaphoreType.DMA
-    pos, vel, pulls, arrived = pl.pallas_call(
+    pos, vel, accel = pl.pallas_call(
         functools.partial(kernel, rows, cols),
         out_shape=(
-            jax.ShapeDtypeStruct(star_pos.shape, F32),
-            jax.ShapeDtypeStruct(star_vel.shape, F32),
-            jax.ShapeDtypeStruct((count, 3 * slots, depth), F32),
-            jax.ShapeDtypeStruct((count, 1, 128), jnp.int32),
+            jax.ShapeDtypeStruct((3, nblock, width), F32),
+            jax.ShapeDtypeStruct((3, nblock, width), F32),
+            jax.ShapeDtypeStruct((3, leaves, depth), F32),
         ),
         in_specs=[vmem] * 6 + [smem] + [vmem] * 3,
-        out_specs=(vmem,) * 4,
+        out_specs=(vmem,) * 3,
         scratch_shapes=[
             pltpu.VMEM((8, stars), F32),
             pltpu.VMEM((8, stars), F32),
@@ -509,17 +508,22 @@
             pltpu.VMEM((cols, nact, 64), BF16),
             pltpu.VMEM((64, stars), BF16),
             pltpu.VMEM((64, stars), BF16),
-            pltpu.VMEM((128, stars), BF16),
+            pltpu.VMEM((stars, 128), BF16),
             pltpu.VMEM((cols, nact, 128), F32),
             pltpu.VMEM((cols, nact, 128), F32),
             pltpu.VMEM((cols, 8, nact), F32),
             pltpu.VMEM((cols, 8, nact), F32),
             pltpu.VMEM((count, 4 * slots, depth), F32),
             pltpu.VMEM((count, 4 * slots, depth), F32),
-            pltpu.VMEM((count, 3 * slots, depth), F32),
+            pltpu.VMEM((count, 4 * slots, depth), F32),
+            pltpu.VMEM((count, 4 * slots, depth), F32),
+            pltpu.VMEM((count, 4 * slots, depth), jnp.int32),
+            pltpu.VMEM((3 * leaves, count * 4 * slots), BF16),
+            pltpu.VMEM((width, 16 * nblock), F32),
             pltpu.VMEM((nblock, width, 64), BF16),
             pltpu.VMEM((nblock, 16, 2 * width), BF16),
             pltpu.VMEM((8, stars), F32),
+            pltpu.VMEM((count, 1, 128), jnp.int32),
             pltpu.SMEM((count, 1, 128), jnp.int32),
             dma((count,)),
             dma((count,)),
@@ -539,29 +543,18 @@
             collective_id=0, has_side_effects=True, vmem_limit_bytes=48 * 1024 * 1024
         ),
     )(
-        star_pos,
-        star_vel,
-        star_acc,
-        star_jerk,
+        star_pos.transpose(1, 0, 2),
+        star_vel.transpose(1, 0, 2),
+        star_acc.transpose(1, 0, 2),
+        star_jerk.transpose(1, 0, 2),
         star_mass,
         active_index,
-        send_block,
+        send_block[0].T,
         lists,
-        galaxy_pos,
+        galaxy_pos.transpose(1, 0, 2),
         galaxy_mass,
     )
-    accel, pos, vel = pl.pallas_call(
-        functools.partial(gather_kernel, float(nblock * count)),
-        out_shape=(
-            jax.ShapeDtypeStruct(galaxy_pos.shape, F32),
-            jax.ShapeDtypeStruct(star_pos.shape, F32),
-            jax.ShapeDtypeStruct(star_vel.shape, F32),
-        ),
-        in_specs=[vmem, smem, vmem, vmem],
-        out_specs=(vmem,) * 3,
-        compiler_params=pltpu.CompilerParams(vmem_limit_bytes=48 * 1024 * 1024),
-    )(pulls, arrived, pos, vel)
-    return (pos, vel, accel)
+    return tuple(x.transpose(1, 0, 2) for x in (pos, vel, accel))
 
 
 def solution(mesh):

time: 69.5 us -> 55.2 us (0.79)
  Pallas kernels: 61.9 us -> 48.9 us
  local copies, waits for them, and re-layouts: 6.54 us -> 5.11 us
    pallas_call x1, Pallas kernels: 59.7 us -> 48.9 us  [local(): pl.pallas_call(functools.partial(kernel, rows, cols), out_shape=(jax.Shap...]
    pallas_call x1 -> x0, Pallas kernels: 2.18 us -> none  [local(): pl.pallas_call(functools.partial(gather_kernel, float(nblock * count)), o...]
    unnamed x25 -> x23, local copies, waits for them, and re-layouts: 6.44 us -> 5.01 us
where the time goes in v2:
time: 55.2 us; the launch traced here: 54.7 us
  Pallas kernels  48.9 us (89%)
  local copies, waits for them, and re-layouts  5.11 us (9%)
  between operations  0.69 us (1%)
    pallas_call x1, Pallas kernels, local(): pl.pallas_call(functools.partial(kernel, rows, cols), out_shape=(jax.Shap...  48.9 us
    unnamed x23, local copies, waits for them, and re-layouts  5.01 us

profile of v2, /device:TPU:1, one launch (start us, length us, event | category | flops | bytes accessed | tf_op | source)
XLA Modules:
  0.0 54.7 jit_solution(259024646613282777)
XLA Ops:
  0.6 0.0 copy-start.9
  0.6 0.7 %copy-done.9 = s32[1,32,4]{1,2,0:T(4,128)S(1)} copy-done((s32[1,32,4]{1,2,0:T(4,128)S(1)}, s32[1,32,4]{1,2,0:T(4,128)}, u32[]{:S(2)}) %copy-start.9) | copy-done | bytes 536
  1.3 0.1 copy.13
  1.4 0.0 copy-start.2
  1.4 0.0 copy-start.3
  1.4 0.0 copy-start.4
  1.4 0.0 copy-start.5
  1.4 0.0 copy-start.6
  1.4 0.0 copy-start.7
  1.4 0.0 copy-start.8
  1.5 0.6 %copy-done.2 = f32[4,3,128]{2,0,1:T(4,128)S(1)} copy-done((f32[4,3,128]{2,0,1:T(4,128)S(1)}, f32[4,3,128]{2,0,1:T(4,128)}, u32[]{:S(2)}) %copy-start.2) | copy-done | bytes 6168
  2.1 0.0 copy-done.3
  2.1 0.0 copy-done.4
  2.1 0.0 copy-done.5
  2.1 0.0 copy-done.6
  2.1 0.0 copy-done.7
  2.2 0.0 copy-done.8
  2.2 0.0 copy-start
  2.2 0.9 %copy-done = f32[128,3,128]{2,0,1:T(8,128)S(1)} copy-done((f32[128,3,128]{2,0,1:T(8,128)S(1)}, f32[128,3,128]{2,0,1:T(8,128)}, u32[]{:S(2)}) %copy-start) | copy-done | bytes 196632
  3.1 0.0 copy-start.1
  3.1 0.8 %copy-done.1 = f32[128,128]{1,0:T(8,128)S(1)} copy-done((f32[128,128]{1,0:T(8,128)S(1)}, f32[128,128]{1,0:T(8,128)}, u32[]{:S(2)}) %copy-start.1) | copy-done | bytes 65560
  3.9 48.9 %shard_map.121 = (f32[3,4,128]{2,1,0:T(4,128)S(1)}, f32[3,4,128]{2,1,0:T(4,128)S(1)}, f32[3,128,128]{2,1,0:T(8,128)S(1)}) custom-call(f32[3,4,128]{2,1,0:T(4,128)S(1)} %bitcast.16, f32[3,4,128]{2,1,0:T(4,128)S(1)} %bitcast.17, f32[3,4,128]{2,1,0:T(4,128)S(1)} %bitcast.18, f32[3,4,128]{2,1,0:T(4,128)S(1)} %bitcast.19, f32[4,128]{1,0:T(4,128)S(1)} %copy-done.6, ...), custom_call_target="tpu_custom_call" | custom-call | tf_op jit(solution)/shard_map/pallas_call | solution.py:493
  52.9 0.6 %copy.17 = f32[4,3,128]{2,0,1:T(4,128)} copy(f32[4,3,128]{2,0,1:T(4,128)S(1)} %bitcast.15) | data formatting | bytes 12288
  53.5 0.6 %copy.18 = f32[4,3,128]{2,0,1:T(4,128)} copy(f32[4,3,128]{2,0,1:T(4,128)S(1)} %bitcast.14) | data formatting | bytes 12288
  54.1 0.7 %copy.19 = f32[128,3,128]{2,0,1:T(8,128)} copy(f32[128,3,128]{2,0,1:T(8,128)S(1)} %bitcast.13) | data formatting | bytes 393216
  (1 shorter events, 0.0 us)
Async XLA Ops:
  0.6 0.7 %copy-start.9 = (s32[1,32,4]{1,2,0:T(4,128)S(1)}, s32[1,32,4]{1,2,0:T(4,128)}, u32[]{:S(2)}) copy-start(s32[1,32,4]{1,2,0:T(4,128)} %param.17) | copy-start | bytes 1540
  1.4 0.7 %copy-start.2 = (f32[4,3,128]{2,0,1:T(4,128)S(1)}, f32[4,3,128]{2,0,1:T(4,128)}, u32[]{:S(2)}) copy-start(f32[4,3,128]{2,0,1:T(4,128)} %param.10) | copy-start | bytes 18436
  1.4 0.7 %copy-start.3 = (f32[4,3,128]{2,0,1:T(4,128)S(1)}, f32[4,3,128]{2,0,1:T(4,128)}, u32[]{:S(2)}) copy-start(f32[4,3,128]{2,0,1:T(4,128)} %param.11) | copy-start | bytes 18436
  1.4 0.7 %copy-start.4 = (f32[4,3,128]{2,0,1:T(4,128)S(1)}, f32[4,3,128]{2,0,1:T(4,128)}, u32[]{:S(2)}) copy-start(f32[4,3,128]{2,0,1:T(4,128)} %param.12) | copy-start | bytes 18436
  1.4 0.7 %copy-start.5 = (f32[4,3,128]{2,0,1:T(4,128)S(1)}, f32[4,3,128]{2,0,1:T(4,128)}, u32[]{:S(2)}) copy-start(f32[4,3,128]{2,0,1:T(4,128)} %param.13) | copy-start | bytes 18436
  1.4 0.7 %copy-start.6 = (f32[4,128]{1,0:T(4,128)S(1)}, f32[4,128]{1,0:T(4,128)}, u32[]{:S(2)}) copy-start(f32[4,128]{1,0:T(4,128)} %smass.1) | copy-start | bytes 6148
  1.4 0.7 %copy-start.7 = (s32[1,32,4]{1,2,0:T(4,128)S(1)}, s32[1,32,4]{1,2,0:T(4,128)}, u32[]{:S(2)}) copy-start(s32[1,32,4]{1,2,0:T(4,128)} %param.16) | copy-start | bytes 1540
  1.4 0.7 %copy-start.8 = (s32[1,128]{1,0:T(1,128)S(1)}, s32[1,128]{1,0:T(1,128)}, u32[]{:S(2)}) copy-start(s32[1,128]{1,0:T(1,128)} %index.1) | copy-start | bytes 1540
  2.2 0.9 %copy-start = (f32[128,3,128]{2,0,1:T(8,128)S(1)}, f32[128,3,128]{2,0,1:T(8,128)}, u32[]{:S(2)}) copy-start(f32[128,3,128]{2,0,1:T(8,128)} %param.18) | copy-start | bytes 589828
  3.1 0.8 %copy-start.1 = (f32[128,128]{1,0:T(8,128)S(1)}, f32[128,128]{1,0:T(8,128)}, u32[]{:S(2)}) copy-start(f32[128,128]{1,0:T(8,128)} %gmass.1) | copy-start | bytes 196612

commit v3 on v2

--- a/solution.py
+++ b/solution.py
@@ -92,8 +92,8 @@
     index,
     sblock,
     lists,
-    gpos,
-    gmass,
+    gpos_hbm,
+    gmass_hbm,
     out_pos,
     out_vel,
     out_accel,
@@ -135,6 +135,9 @@
     pull_send,
     pull_recv,
     local_sem,
+    all_here,
+    gpos,
+    gmass,
 ):
     mr = lax.axis_index("row")
     mc = lax.axis_index("col")
@@ -150,13 +153,30 @@
 
     barrier = pltpu.get_barrier_semaphore()
 
-    def greet(off, carry):
+    def greet_col(off, carry):
         pl.semaphore_signal(
-            barrier, inc=1, device_id=where_is((me + off) % count), device_id_type=MESH
+            barrier, inc=1, device_id=(mr, (mc + off) % cols), device_id_type=MESH
         )
         return carry
 
-    lax.fori_loop(1, count, greet, 0)
+    def greet_row(off, carry):
+        pl.semaphore_signal(
+            barrier, inc=1, device_id=((mr + off) % rows, mc), device_id_type=MESH
+        )
+        return carry
+
+    def vouch(off, carry):
+        pl.semaphore_signal(
+            all_here, inc=1, device_id=((mr + off) % rows, mc), device_id_type=MESH
+        )
+        return carry
+
+    lax.fori_loop(1, cols, greet_col, 0)
+    lax.fori_loop(1, rows, greet_row, 0)
+    fetch_pos = pltpu.make_async_copy(gpos_hbm, gpos, local_sem.at[1])
+    fetch_mass = pltpu.make_async_copy(gmass_hbm, gmass, local_sem.at[2])
+    fetch_pos.start()
+    fetch_mass.start()
 
     base_a[...] = jnp.zeros_like(base_a)
     base_b[...] = jnp.zeros_like(base_b)
@@ -187,7 +207,8 @@
     )
     act_all[mc] = mine
 
-    pl.semaphore_wait(barrier, count - 1)
+    pl.semaphore_wait(barrier, cols + rows - 2)
+    lax.fori_loop(1, rows, vouch, 0)
 
     def act_copy(peer, slot):
         return pltpu.make_async_remote_copy(
@@ -258,7 +279,6 @@
 
     each(cols, mc, lambda peer: act_copy(peer, mc).start())
     each(rows, mr, lambda peer: star_copy(peer, mr).start())
-    each(count, me, lambda peer: list_copy(peer, me).start())
     lists_in[me] = lists[me]
 
     def prepare(r):
@@ -277,6 +297,8 @@
         high, low = split2(jnp.where(body, table * mass, jnp.where(row == 3, mass, 0.0)))
         pad = jnp.zeros((weigh.shape[1] - 16, stars), F32)
         weigh[...] = jnp.concatenate([high, low, pad], 0).T.astype(BF16)
+
+    group = 2 if cols % 2 == 0 else 1
 
     def pairs(c):
         lhs = left[c]
@@ -299,6 +321,8 @@
     acc_q[...] = jnp.zeros_like(acc_q)
     prepare(mr)
     left_of(mc)
+    pl.semaphore_wait(all_here, rows - 1)
+    each(count, me, lambda peer: list_copy(peer, me).start())
     pairs(mc)
 
     def take_active(off, carry):
@@ -311,7 +335,9 @@
     lax.fori_loop(1, cols, take_active, 0)
 
     each(count, me, lambda peer: list_copy(peer, peer).wait_recv())
-    move = pltpu.make_async_copy(lists_in, lists_s, local_sem)
+    move = pltpu.make_async_copy(lists_in, lists_s, local_sem.at[0])
+    fetch_pos.wait()
+    fetch_mass.wait()
     move.start()
     move.wait()
 
@@ -347,10 +373,11 @@
         prepare(r)
 
         def inner(c, carry):
-            pairs(c)
+            for k in range(group):
+                pairs(c * group + k)
             return carry
 
-        lax.fori_loop(0, cols, inner, 0)
+        lax.fori_loop(0, cols // group, inner, 0)
         return carry
 
     lax.fori_loop(1, rows, take_stars, 0)
@@ -401,10 +428,10 @@
         both = jnp.concatenate([high, low], 0).astype(BF16)
         sfeat[b] = jnp.concatenate([both, both], 1)
 
-    def entries(peer, ref):
+    def entries(work_list):
         weights = []
         feats = []
-        for s in range(slots):
+        for peer, ref, s in [(p, q, s) for p, q in work_list for s in range(slots)]:
             block = sblock[s, peer]
             at = jnp.maximum(block, 0)
             leaf = leaves_in[peer, 4 * s : 4 * s + 4, :]
@@ -430,16 +457,23 @@
             ref[peer, 4 * s : 4 * s + 4, :] = pull[0:4]
         kicks[...] += dot_t(jnp.concatenate(weights, 1), jnp.concatenate(feats, 1))
 
-    def work(off, carry):
-        peer = (me + off) % count
+    def work(step, carry):
+        peers = [(me + 2 * step + k) % count for k in (1, 2)]
+        for peer in peers:
+            leaf_copy(peer, peer).wait_recv()
+        entries([(peer, pull_out) for peer in peers])
+        for peer in peers:
+            pull_copy(peer, me).start()
+        return carry
+
+    kicks[...] = jnp.zeros_like(kicks)
+    lax.fori_loop(0, (count - 1) // 2, work, 0)
+    rest = [(me + off) % count for off in range(1 + 2 * ((count - 1) // 2), count)]
+    for peer in rest:
         leaf_copy(peer, peer).wait_recv()
-        entries(peer, pull_out)
+    entries([(peer, pull_out) for peer in rest] + [(me, pulls)])
+    for peer in rest:
         pull_copy(peer, me).start()
-        return carry
-
-    kicks[...] = jnp.zeros_like(kicks)
-    lax.fori_loop(1, count, work, 0)
-    entries(me, pulls)
     turned = kicks[...].T
     for b in range(nblock):
         table = fresh[:, pl.ds(b * width, width)]
@@ -489,6 +523,7 @@
     lists = jnp.pad(send_leaf[0][:, None, :], ((0, 0), (0, 0), (0, 128 - slots)))
     vmem = pl.BlockSpec(memory_space=pltpu.VMEM)
     smem = pl.BlockSpec(memory_space=pltpu.SMEM)
+    hbm = pl.BlockSpec(memory_space=pltpu.HBM)
     dma = pltpu.SemaphoreType.DMA
     pos, vel, accel = pl.pallas_call(
         functools.partial(kernel, rows, cols),
@@ -497,7 +532,7 @@
             jax.ShapeDtypeStruct((3, nblock, width), F32),
             jax.ShapeDtypeStruct((3, leaves, depth), F32),
         ),
-        in_specs=[vmem] * 6 + [smem] + [vmem] * 3,
+        in_specs=[vmem] * 6 + [smem, vmem, hbm, hbm],
         out_specs=(vmem,) * 3,
         scratch_shapes=[
             pltpu.VMEM((8, stars), F32),
@@ -537,7 +572,10 @@
             dma((cols,)),
             dma((count,)),
             dma((count,)),
-            dma(()),
+            dma((3,)),
+            pltpu.SemaphoreType.REGULAR,
+            pltpu.VMEM((3, leaves, depth), F32),
+            pltpu.VMEM((leaves, depth), F32),
         ],
         compiler_params=pltpu.CompilerParams(
             collective_id=0, has_side_effects=True, vmem_limit_bytes=48 * 1024 * 1024

time: 55.2 us -> 49.1 us (0.89)
  Pallas kernels: 48.9 us -> 43 us
    pallas_call x1, Pallas kernels: 48.9 us -> 43 us  [local(): pl.pallas_call(functools.partial(kernel, rows, cols), out_shape=(jax.Shap...]
where the time goes in v3:
time: 49.1 us; the launch traced here: 48.8 us
  Pallas kernels  43 us (88%)
  local copies, waits for them, and re-layouts  5.11 us (10%)
  between operations  0.69 us (1%)
    pallas_call x1, Pallas kernels, local(): pl.pallas_call(functools.partial(kernel, rows, cols), out_shape=(jax.Shap...  43 us
    unnamed x23, local copies, waits for them, and re-layouts  5.01 us

profile of v3, /device:TPU:1, one launch (start us, length us, event | category | flops | bytes accessed | tf_op | source)
XLA Modules:
  0.0 48.8 jit_solution(9931431657566907288)
XLA Ops:
  0.6 0.0 copy-start.9
  0.6 0.7 %copy-done.9 = s32[1,32,4]{1,2,0:T(4,128)S(1)} copy-done((s32[1,32,4]{1,2,0:T(4,128)S(1)}, s32[1,32,4]{1,2,0:T(4,128)}, u32[]{:S(2)}) %copy-start.9) | copy-done | bytes 536
  1.3 0.1 copy.13
  1.4 0.0 copy-start.2
  1.4 0.0 copy-start.3
  1.4 0.0 copy-start.4
  1.4 0.0 copy-start.5
  1.4 0.0 copy-start.6
  1.4 0.0 copy-start.7
  1.4 0.0 copy-start.8
  1.5 0.6 %copy-done.2 = f32[4,3,128]{2,0,1:T(4,128)S(1)} copy-done((f32[4,3,128]{2,0,1:T(4,128)S(1)}, f32[4,3,128]{2,0,1:T(4,128)}, u32[]{:S(2)}) %copy-start.2) | copy-done | bytes 6168
  2.1 0.0 copy-done.3
  2.1 0.0 copy-done.4
  2.1 0.0 copy-done.5
  2.1 0.0 copy-done.6
  2.1 0.0 copy-done.7
  2.2 0.0 copy-done.8
  2.2 0.0 copy-start
  2.2 0.9 %copy-done = f32[128,3,128]{2,0,1:T(8,128)S(1)} copy-done((f32[128,3,128]{2,0,1:T(8,128)S(1)}, f32[128,3,128]{2,0,1:T(8,128)}, u32[]{:S(2)}) %copy-start) | copy-done | bytes 196632
  3.1 0.0 copy-start.1
  3.1 0.8 %copy-done.1 = f32[128,128]{1,0:T(8,128)S(1)} copy-done((f32[128,128]{1,0:T(8,128)S(1)}, f32[128,128]{1,0:T(8,128)}, u32[]{:S(2)}) %copy-start.1) | copy-done | bytes 65560
  3.9 43.0 %shard_map.121 = (f32[3,4,128]{2,1,0:T(4,128)S(1)}, f32[3,4,128]{2,1,0:T(4,128)S(1)}, f32[3,128,128]{2,1,0:T(8,128)S(1)}) custom-call(f32[3,4,128]{2,1,0:T(4,128)S(1)} %bitcast.16, f32[3,4,128]{2,1,0:T(4,128)S(1)} %bitcast.17, f32[3,4,128]{2,1,0:T(4,128)S(1)} %bitcast.18, f32[3,4,128]{2,1,0:T(4,128)S(1)} %bitcast.19, f32[4,128]{1,0:T(4,128)S(1)} %copy-done.6, ...), custom_call_target="tpu_custom_call" | custom-call | tf_op jit(solution)/shard_map/pallas_call | solution.py:528
  46.9 0.6 %copy.17 = f32[4,3,128]{2,0,1:T(4,128)} copy(f32[4,3,128]{2,0,1:T(4,128)S(1)} %bitcast.15) | data formatting | bytes 12288
  47.5 0.6 %copy.18 = f32[4,3,128]{2,0,1:T(4,128)} copy(f32[4,3,128]{2,0,1:T(4,128)S(1)} %bitcast.14) | data formatting | bytes 12288
  48.1 0.7 %copy.19 = f32[128,3,128]{2,0,1:T(8,128)} copy(f32[128,3,128]{2,0,1:T(8,128)S(1)} %bitcast.13) | data formatting | bytes 393216
  (1 shorter events, 0.0 us)
Async XLA Ops:
  0.6 0.7 %copy-start.9 = (s32[1,32,4]{1,2,0:T(4,128)S(1)}, s32[1,32,4]{1,2,0:T(4,128)}, u32[]{:S(2)}) copy-start(s32[1,32,4]{1,2,0:T(4,128)} %param.17) | copy-start | bytes 1540
  1.4 0.7 %copy-start.2 = (f32[4,3,128]{2,0,1:T(4,128)S(1)}, f32[4,3,128]{2,0,1:T(4,128)}, u32[]{:S(2)}) copy-start(f32[4,3,128]{2,0,1:T(4,128)} %param.10) | copy-start | bytes 18436
  1.4 0.7 %copy-start.3 = (f32[4,3,128]{2,0,1:T(4,128)S(1)}, f32[4,3,128]{2,0,1:T(4,128)}, u32[]{:S(2)}) copy-start(f32[4,3,128]{2,0,1:T(4,128)} %param.11) | copy-start | bytes 18436
  1.4 0.7 %copy-start.4 = (f32[4,3,128]{2,0,1:T(4,128)S(1)}, f32[4,3,128]{2,0,1:T(4,128)}, u32[]{:S(2)}) copy-start(f32[4,3,128]{2,0,1:T(4,128)} %param.12) | copy-start | bytes 18436
  1.4 0.7 %copy-start.5 = (f32[4,3,128]{2,0,1:T(4,128)S(1)}, f32[4,3,128]{2,0,1:T(4,128)}, u32[]{:S(2)}) copy-start(f32[4,3,128]{2,0,1:T(4,128)} %param.13) | copy-start | bytes 18436
  1.4 0.7 %copy-start.6 = (f32[4,128]{1,0:T(4,128)S(1)}, f32[4,128]{1,0:T(4,128)}, u32[]{:S(2)}) copy-start(f32[4,128]{1,0:T(4,128)} %smass.1) | copy-start | bytes 6148
  1.4 0.7 %copy-start.7 = (s32[1,32,4]{1,2,0:T(4,128)S(1)}, s32[1,32,4]{1,2,0:T(4,128)}, u32[]{:S(2)}) copy-start(s32[1,32,4]{1,2,0:T(4,128)} %param.16) | copy-start | bytes 1540
  1.4 0.7 %copy-start.8 = (s32[1,128]{1,0:T(1,128)S(1)}, s32[1,128]{1,0:T(1,128)}, u32[]{:S(2)}) copy-start(s32[1,128]{1,0:T(1,128)} %index.1) | copy-start | bytes 1540
  2.2 0.9 %copy-start = (f32[128,3,128]{2,0,1:T(8,128)S(1)}, f32[128,3,128]{2,0,1:T(8,128)}, u32[]{:S(2)}) copy-start(f32[128,3,128]{2,0,1:T(8,128)} %param.18) | copy-start | bytes 589828
  3.1 0.8 %copy-start.1 = (f32[128,128]{1,0:T(8,128)S(1)}, f32[128,128]{1,0:T(8,128)}, u32[]{:S(2)}) copy-start(f32[128,128]{1,0:T(8,128)} %gmass_hbm.1) | copy-start | bytes 196612
